TPU v7x, 32 devices: a whole 2x2x4 slice. The times are simulated.
32 devices in a mesh: vocab: 4 (over y, core), dp: 2 (over x), replica: 4 (over z).
Axes of the slice: x: 2, y: 2, z: 4, core: 2. Of those that a mesh axis runs over, the one named last changes fastest.
Arguments:
- hidden: bfloat16 [256, 4096], P('dp'), may hold values from -6 to 6
- head_weight: bfloat16 [4096, 16384], P('dp', ('vocab', 'replica')), may hold values from -0.09375 to 0.09375
- head_bias: float32 [16384], P(('vocab', 'replica')), may hold values from -2.5 to 2.5
- rep_cotangent: float32 [16, 16384], P('dp', ('vocab', 'replica')), may hold values from -6 to 6
- lengths: int32 [16], P('dp'), may hold values from 1 to 16, 160 in all
Outputs:
- pooled: float32 [16, 16384], P('dp', ('vocab', 'replica'))
- term_mean: float32 [16384], P(('vocab', 'replica'))
- bias_grad: float32 [16384], P(('vocab', 'replica'))
- weight_grad: float32 [4096, 16384], P('dp', ('vocab', 'replica'))
- input_grad: float32 [256, 4096], P(('vocab', 'replica'), 'dp')
Inputs may be any that keep to these rules, and one draw needn't show every extreme that they name: `lengths`: each sequence has at least one live token; some sequence has all 16 live.
All inputs are finite; a program needn't handle non-finite values. No bound on the sum of `lengths` on one device may be relied on, other than what follows from the above.
Results may differ from a plain program's by a relative error of at most 0.015.
Values may be sent and summed in bfloat16 or wider, within the bound.
A program may use at most 64 MiB of HBM per device.

v0:
```python
import jax
import jax.numpy as jnp
from jax import lax
from jax.sharding import PartitionSpec as P


def per_device(hidden, head_weight, head_bias, rep_cotangent, lengths):
    tok_rows = hidden.shape[0]
    block = head_weight.shape[0]
    vocab_cols = head_weight.shape[1]
    dp_count = lax.axis_size("dp")
    seq_count = lengths.shape[0]
    seq_len = tok_rows // seq_count
    columns = lax.all_to_all(hidden, "dp", split_axis=1, concat_axis=0, tiled=True)
    running = jnp.zeros((tok_rows, vocab_cols), jnp.float32)
    piece = lax.all_gather(head_weight, "dp", axis=0, tiled=True)
    count = piece.shape[0] // block
    for index in range(count):
        left = lax.dynamic_slice_in_dim(hidden, index * block, block, 1)
        part = jnp.dot(
            left, piece[index * block : (index + 1) * block, :], preferred_element_type=jnp.float32
        ).astype(jnp.bfloat16)
        running = running + lax.optimization_barrier(part).astype(jnp.float32)
    logits = running + head_bias[None, :]
    positive = jnp.maximum(logits, 0.0)
    grid = jnp.log1p(positive).reshape(seq_count, seq_len, vocab_cols)
    live = (jnp.arange(seq_len, dtype=jnp.int32)[None, :] < lengths[:, None]).astype(jnp.float32)[
        :, :, None
    ]
    squared = grid * grid
    total = 1.0 + jnp.sum(live * squared * squared, axis=1)
    pooled = total**0.25 - 1.0
    factor = (
        live
        * squared
        * grid
        * (total ** (-0.75))[:, None, :]
        / (1.0 + positive.reshape(seq_count, seq_len, vocab_cols))
    )
    column_sum = jnp.sum(pooled, axis=0)
    seq_total = seq_count * dp_count
    term_mean = lax.psum(column_sum, "dp") / seq_total
    grad_pooled = rep_cotangent + term_mean[None, :]
    grad_logits = (factor * grad_pooled[:, None, :]).reshape(tok_rows, vocab_cols)
    bias_grad = lax.psum(jnp.sum(grad_logits, axis=0), "dp")
    grad_round = grad_logits.astype(jnp.bfloat16)
    piece = lax.all_gather(grad_round, "dp", axis=0, tiled=True)
    left = columns
    weight_sum_acc = jnp.einsum("tk,tv->kv", left, piece, preferred_element_type=jnp.float32)
    rows_out = jnp.einsum("tv,kv->tk", piece, head_weight, preferred_element_type=jnp.float32)
    input_part = rows_out
    weight_grad, input_part = (weight_sum_acc, input_part)
    input_grad = lax.psum_scatter(input_part, ("vocab", "replica"), scatter_dimension=0, tiled=True)
    return (pooled, term_mean, bias_grad, weight_grad, input_grad)


def solution(mesh):
    placed = (
        P("dp", None),
        P("dp", ("vocab", "replica")),
        P(("vocab", "replica")),
        P("dp", ("vocab", "replica")),
        P("dp"),
    )
    return jax.shard_map(
        per_device,
        mesh=mesh,
        in_specs=placed,
        out_specs=(
            P("dp", ("vocab", "replica")),
            P(("vocab", "replica")),
            P(("vocab", "replica")),
            P("dp", ("vocab", "replica")),
            P(("vocab", "replica"), "dp"),
        ),
        check_vma=False,
    )
```

profile of v0, /device:TPU:0, one launch (start us, length us, event | category | flops | bytes accessed | tf_op | source)
XLA Modules:
  0.0 209.5 jit_solution(16055602566687001049)
XLA Ops:
  7.2 0.0 copy-start.4
  7.2 0.0 copy-start
  7.2 0.0 all-gather.2.cloned.1.call-start
  7.2 0.7 all-gather.2.cloned.1.call-update
  7.9 0.0 reduce-scatter.2.cloned.1.call-start
  8.0 0.0 copy-done.4
  8.0 0.1 fusion.14
  8.0 0.1 reshape.55
  8.1 108.2 %all-gather.2.cloned.1.call-done = bf16[4096,1024]{1,0:T(8,128)(2,1)} async-done(((bf16[2048,1024]{1,0:T(8,128)(2,1)}), bf16[4096,1024]{1,0:T(8,128)(2,1)}) %all-gather.2.cloned.1.call-update) | async-done | bytes 8388624 | tf_op jit(solution)/shard_map/all_gather | solution.py:16
  116.3 0.0 copy-done
  116.3 2.9 %fusion.4 = bf16[128,1024]{1,0:T(8,128)(2,1)S(1)} fusion(bf16[4096,1024]{1,0:T(8,128)(2,1)} %all-gather.2.cloned.1.call-done, bf16[128,4096]{1,0:T(8,128)(2,1)S(1)} %copy-done), kind=kOutput, calls=%fused_computation.5 | convolution fusion | flops 537001984 | bytes 4980736 | tf_op jit(solution)/shard_map/dot_general | solution.py:20
  119.2 0.0 copy-start.2
  119.2 0.0 copy-start.1
  119.2 2.9 %fusion.7 = bf16[128,1024]{1,0:T(8,128)(2,1)S(1)} fusion(bf16[4096,1024]{1,0:T(8,128)(2,1)} %all-gather.2.cloned.1.call-done, bf16[128,4096]{1,0:T(8,128)(2,1)S(1)} %copy-done), kind=kOutput, calls=%fused_computation.6 | convolution fusion | flops 537001984 | bytes 4980736 | tf_op jit(solution)/shard_map/dot_general | solution.py:20
  122.2 0.0 copy-done.2
  122.2 0.4 fusion.10
  122.5 0.6 fusion.16
  123.2 4.9 %psum.14 = f32[1024]{0:T(1024)S(1)} all-reduce(f32[1024]{0:T(1024)S(1)} %get-tuple-element.22), channel_id=1, replica_groups=mesh['vocab'=4,'dp'=2,'replica'=4] {'dp'}, use_global_device_ids=true, to_apply=%region_2.0 | all-reduce | flops 1024 | bytes 8192 | tf_op jit(solution)/shard_map/psum | solution.py:42
  128.1 0.0 copy-done.1
  128.1 0.0 copy-start.3
  128.1 0.4 fusion.15
  128.5 7.6 %all_gather.7 = bf16[256,1024]{1,0:T(8,128)(2,1)S(1)} all-gather(bf16[128,1024]{1,0:T(8,128)(2,1)S(1)} %get-tuple-element.20), channel_id=1, replica_groups=mesh['vocab'=4,'dp'=2,'replica'=4] {'dp'}, dimensions={0}, use_global_device_ids=true | all-gather | bytes 786432 | tf_op jit(solution)/shard_map/all_gather | solution.py:47
  136.1 4.9 %fusion.17 = f32[256,2048]{1,0:T(8,128)} fusion(bf16[256,1024]{1,0:T(8,128)(2,1)S(1)} %all_gather.7, bf16[2048,1024]{1,0:T(8,128)(2,1)} %param.6), kind=kOutput, calls=%fused_computation.24 | convolution fusion | flops 1073741824 | bytes 6815744 | tf_op jit(solution)/shard_map/tv,kv->tk/dot_general | solution.py:50
  140.9 0.0 copy-done.3
  140.9 0.0 reduce-scatter.2.cloned.1.call-update
  141.0 0.7 copy.12
  141.6 14.3 %all_to_all.19 = bf16[128,2,2048]{0,2,1:T(8,128)(2,1)S(1)} all-to-all(bf16[128,2,2048]{0,2,1:T(8,128)(2,1)S(1)} %bitcast.23), channel_id=1, replica_groups=mesh['vocab'=4,'dp'=2,'replica'=4] {'dp'}, dimensions={1} | all-to-all | bytes 2097152 | tf_op jit(solution)/shard_map/all_to_all | solution.py:14
  155.9 0.5 copy.13
  156.4 4.5 %convolution_bitcast_fusion = f32[2048,1024]{0,1:T(8,128)} fusion(bf16[256,1024]{1,0:T(8,128)(2,1)S(1)} %all_gather.7, bf16[256,2048]{1,0:T(8,128)(2,1)S(1)} %bitcast.21), kind=kOutput, calls=%fused_computation | convolution fusion | flops 1073741824 | bytes 9961472 | tf_op jit(solution)/shard_map/tk,tv->kv/dot_general | solution.py:49
  160.9 9.2 %copy.14 = f32[2048,1024]{1,0:T(8,128)} copy(f32[2048,1024]{0,1:T(8,128)} %convolution_bitcast_fusion) | data formatting | bytes 16777216
  170.2 5.5 %psum.15 = f32[1024]{0:T(1024)} all-reduce(f32[1024]{0:T(1024)S(1)} %reduce_sum.29), channel_id=1, replica_groups=mesh['vocab'=4,'dp'=2,'replica'=4] {'dp'}, use_global_device_ids=true, to_apply=%region_4.0 | all-reduce | flops 1024 | bytes 8192 | tf_op jit(solution)/shard_map/psum | solution.py:45
  175.8 26.9 %reduce-scatter.2.cloned.1.call-done = f32[16,2048]{1,0:T(8,128)} async-done(((f32[256,2048]{1,0:T(8,128)}), f32[16,2048]{1,0:T(8,128)}) %reduce-scatter.2.cloned.1.call-update) | async-done | bytes 131088 | tf_op jit(solution)/shard_map/reduce_scatter | solution.py:53
  (3 shorter events, 0.1 us)
Async XLA Ops:
  7.2 0.8 copy-start.4
  7.2 109.1 %copy-start = (bf16[128,4096]{1,0:T(8,128)(2,1)S(1)}, bf16[128,4096]{1,0:T(8,128)(2,1)}, u32[]{:S(2)}) copy-start(bf16[128,4096]{1,0:T(8,128)(2,1)} %param.5) | copy-start | bytes 3145732
  7.2 109.1 %all-gather.2.cloned.1.call-start = ((), (), s32[]{:S(2)}) async-start(), calls=%async_computation.2 | async-start | bytes 12582912 | tf_op jit(solution)/shard_map/all_gather | solution.py:16
  7.9 194.8 %reduce-scatter.2.cloned.1.call-start = ((), (), s32[]{:S(2)}) async-start(), calls=%async_computation.3 | async-start | bytes 2228224 | tf_op jit(solution)/shard_map/reduce_scatter | solution.py:53
  119.2 2.9 %copy-start.2 = (f32[1024]{0:T(1024)S(1)}, f32[1024]{0:T(1024)}, u32[]{:S(2)}) copy-start(f32[1024]{0:T(1024)} %param.7) | copy-start | bytes 12292
  119.2 8.9 %copy-start.1 = (f32[8,1024]{1,0:T(8,128)S(1)}, f32[8,1024]{1,0:T(8,128)}, u32[]{:S(2)}) copy-start(f32[8,1024]{1,0:T(8,128)} %param.8) | copy-start | bytes 98308
  128.1 12.8 %copy-start.3 = (f32[1024]{0:T(1024)}, f32[1024]{0:T(1024)S(1)}, u32[]{:S(2)}) copy-start(f32[1024]{0:T(1024)S(1)} %broadcast_multiply_fusion) | copy-start | bytes 12292
Sparse Core Ops, SparseCore 0:
  9.6 106.6 all-gather.1
  141.1 61.5 reduce-scatter.1
where the time goes:
time: 210 us
  waiting for transfers between devices  136 us (65%)
  blocking collectives  32.3 us (15%)
  matrix products  15.2 us (7%)
  between operations  14.1 us (7%)
  local copies, waits for them, and re-layouts  10.5 us (5%)
    all_gather x1, waiting for transfers between devices, per_device(): piece = lax.all_gather(head_weight, 'dp', axis=0, tiled=True)  108 us
    reduce_scatter x1, waiting for transfers between devices, per_device(): lax.psum_scatter(input_part, ('vocab', 'replica'), scatter_dimension=0, t...  26.9 us
    all_to_all x1, blocking collectives, per_device(): lax.all_to_all(hidden, 'dp', split_axis=1, concat_axis=0, tiled=True)  14.3 us
    unnamed x12, local copies, waits for them, and re-layouts  9.93 us
    all_gather x1, blocking collectives, per_device(): piece = lax.all_gather(grad_round, 'dp', axis=0, tiled=True)  7.57 us
    dot_general x2, matrix products, per_device(): jnp.dot(left, piece[index * block:(index + 1) * block, :], preferred_elem...  5.81 us
    psum x1, blocking collectives, per_device(): bias_grad = lax.psum(jnp.sum(grad_logits, axis=0), 'dp')  5.53 us
    psum x1, blocking collectives, per_device(): term_mean = lax.psum(column_sum, 'dp') / seq_total  4.91 us
  transfers between devices with their start and end apart: 2, of which 2 were waited for; matrix products, arithmetic and copies ran while one was open for 7% of the time, Pallas kernels for 0%

commit v1 on v0

v1 whole, which is shorter than its diff:
```python
import jax
import jax.numpy as jnp
from jax import lax
from jax.sharding import PartitionSpec as P


def per_device(hidden, head_weight, head_bias, rep_cotangent, lengths):
    dp_count = lax.axis_size("dp")
    vocab_cols = head_weight.shape[1]
    columns = lax.all_to_all(hidden, "dp", split_axis=1, concat_axis=0, tiled=True)
    rep_all = lax.all_gather(rep_cotangent, "dp", axis=0, tiled=True)
    lengths_all = lax.all_gather(lengths.astype(jnp.float32), "dp", axis=0, tiled=True)
    seq_count = lengths_all.shape[0]
    tok_rows = columns.shape[0]
    seq_len = tok_rows // seq_count
    part = jnp.dot(columns, head_weight, preferred_element_type=jnp.float32).astype(jnp.bfloat16)
    part = lax.optimization_barrier(part)
    if dp_count == 2:
        other = lax.ppermute(part, "dp", [(0, 1), (1, 0)])
        running = part.astype(jnp.float32) + other.astype(jnp.float32)
    else:
        parts = lax.all_gather(part, "dp", axis=0, tiled=False)
        running = jnp.sum(parts.astype(jnp.float32), axis=0)
    logits = running + head_bias[None, :]
    positive = jnp.maximum(logits, 0.0)
    grid = jnp.log1p(positive).reshape(seq_count, seq_len, vocab_cols)
    slot = jnp.arange(seq_len, dtype=jnp.float32)
    live = (slot[None, :] < lengths_all[:, None]).astype(jnp.float32)[:, :, None]
    squared = grid * grid
    total = 1.0 + jnp.sum(live * squared * squared, axis=1)
    pooled = total**0.25 - 1.0
    factor = (
        live * squared * grid * (total ** (-0.75))[:, None, :]
        / (1.0 + positive.reshape(seq_count, seq_len, vocab_cols))
    )
    term_mean = jnp.sum(pooled, axis=0) / seq_count
    grad_pooled = rep_all + term_mean[None, :]
    grad_logits = (factor * grad_pooled[:, None, :]).reshape(tok_rows, vocab_cols)
    bias_grad = jnp.sum(grad_logits, axis=0)
    grad_round = grad_logits.astype(jnp.bfloat16)
    input_part = jnp.einsum("tv,kv->tk", grad_round, head_weight, preferred_element_type=jnp.float32)
    input_grad = lax.psum_scatter(input_part, ("vocab", "replica"), scatter_dimension=0, tiled=True)
    weight_grad = jnp.einsum("tk,tv->kv", columns, grad_round, preferred_element_type=jnp.float32)
    own = seq_count // dp_count
    pooled_own = lax.dynamic_slice_in_dim(pooled, lax.axis_index("dp") * own, own, 0)
    return (pooled_own, term_mean, bias_grad, weight_grad, input_grad)


def solution(mesh):
    placed = (
        P("dp", None),
        P("dp", ("vocab", "replica")),
        P(("vocab", "replica")),
        P("dp", ("vocab", "replica")),
        P("dp"),
    )
    return jax.shard_map(
        per_device,
        mesh=mesh,
        in_specs=placed,
        out_specs=(
            P("dp", ("vocab", "replica")),
            P(("vocab", "replica")),
            P(("vocab", "replica")),
            P("dp", ("vocab", "replica")),
            P(("vocab", "replica"), "dp"),
        ),
        check_vma=False,
    )
```

time: 210 us -> 125 us (0.60)
  waiting for transfers between devices: 136 us -> 48 us
  local copies, waits for them, and re-layouts: 10.5 us -> 12.8 us
  matrix products: 15.2 us -> 12.9 us
    all_gather x1 -> x0, waiting for transfers between devices: 108 us -> none  [per_device(): piece = lax.all_gather(head_weight, 'dp', axis=0, tiled=True)]
    reduce_scatter x1, waiting for transfers between devices: 26.9 us -> 48 us  [per_device(): lax.psum_scatter(input_part, ('vocab', 'replica'), scatter_dimension=0, t...]
    unnamed x0 -> x1, blocking collectives: none -> 10.9 us
    psum x2 -> x0, blocking collectives: 10.4 us -> none  [the longest x1 5.53 us: per_device(): bias_grad = lax.psum(jnp.sum(grad_logits, axis=0), 'dp')]
    all_to_all x1, blocking collectives: 14.3 us -> 17.6 us  [per_device(): lax.all_to_all(hidden, 'dp', split_axis=1, concat_axis=0, tiled=True)]
    all_gather x1, blocking collectives: 7.57 us -> 4.58 us  [per_device(): rep_all = lax.all_gather(rep_cotangent, 'dp', axis=0, tiled=True)]
    dot_general x4 -> x3, matrix products: 15.2 us -> 12.9 us  [the longest x1 4.92 us: per_device(): jnp.einsum('tv,kv->tk', grad_round, head_weight, preferred_element_type=j...]
    unnamed x12 -> x14, local copies, waits for them, and re-layouts: 9.93 us -> 11.6 us
  transfers between devices with their start and end apart: 2 -> 2, of which waited for: 2 -> 1; matrix products, arithmetic and copies ran while one was open for 7% -> 12% of each run, Pallas kernels for 0% -> 0%
where the time goes in v1:
time: 125 us; the launch traced here: 124 us
  waiting for transfers between devices  48 us (38%)
  blocking collectives  33.1 us (26%)
  between operations  14.8 us (12%)
  matrix products  12.9 us (10%)
  local copies, waits for them, and re-layouts  12.8 us (10%)
  other arithmetic  2.37 us (2%)
    reduce_scatter x1, waiting for transfers between devices, per_device(): lax.psum_scatter(input_part, ('vocab', 'replica'), scatter_dimension=0, t...  48 us
    all_to_all x1, blocking collectives, per_device(): lax.all_to_all(hidden, 'dp', split_axis=1, concat_axis=0, tiled=True)  17.6 us
    unnamed x14, local copies, waits for them, and re-layouts  11.6 us
    unnamed x1, blocking collectives  10.9 us
    dot_general x1, matrix products, per_device(): jnp.einsum('tv,kv->tk', grad_round, head_weight, preferred_element_type=j...  4.92 us
    all_gather x1, blocking collectives, per_device(): rep_all = lax.all_gather(rep_cotangent, 'dp', axis=0, tiled=True)  4.58 us
    dot_general x1, matrix products, per_device(): jnp.einsum('tk,tv->kv', columns, grad_round, preferred_element_type=jnp.f...  4.53 us
    dot_general x1, matrix products, per_device(): jnp.dot(columns, head_weight, preferred_element_type=jnp.float32)  3.45 us
  transfers between devices with their start and end apart: 2, of which 1 were waited for; matrix products, arithmetic and copies ran while one was open for 12% of the time, Pallas kernels for 0%

profile of v1, /device:TPU:0, one launch (start us, length us, event | category | flops | bytes accessed | tf_op | source)
XLA Modules:
  0.0 124.4 jit_solution(18241254868801271478)
XLA Ops:
  7.2 0.0 reduce-scatter.2.cloned.1.call-start
  7.2 1.6 %copy.12 = bf16[128,4096]{0,1:T(8,128)(2,1)S(1)} copy(bf16[128,4096]{1,0:T(8,128)(2,1)} %param.5) | data formatting | bytes 2097152 | tf_op args[0]
  8.8 17.6 %all_to_all.19 = bf16[128,2,2048]{0,2,1:T(8,128)(2,1)S(1)} all-to-all(bf16[128,2,2048]{0,2,1:T(8,128)(2,1)S(1)} %bitcast.27), channel_id=1, replica_groups=mesh['vocab'=4,'dp'=2,'replica'=4] {'dp'}, dimensions={1} | all-to-all | bytes 2097152 | tf_op jit(solution)/shard_map/all_to_all | solution.py:10
  26.4 0.5 copy.13
  27.0 0.0 copy-start.4
  27.0 0.0 copy-start.3
  27.0 0.0 copy-start
  27.0 0.0 copy-start.1
  27.0 3.5 %convolution_convert_fusion = bf16[256,1024]{1,0:T(8,128)(2,1)S(1)} fusion(bf16[256,2048]{1,0:T(8,128)(2,1)S(1)} %bitcast.24, bf16[2048,1024]{1,0:T(8,128)(2,1)} %param.6), kind=kOutput, calls=%fused_computation.2 | convolution fusion | flops 1074003968 | bytes 5767168 | tf_op jit(solution)/shard_map/dot_general | solution.py:16
  30.5 0.3 collective-permute-start
  30.8 0.0 copy-done.4
  30.8 0.6 dynamic-slice
  32.1 0.0 copy-done.3
  32.1 0.1 convert_dynamic-update-slice_fusion
  32.2 10.9 %all-reduce = f32[16]{0:T(128)S(1)} all-reduce(f32[16]{0:T(128)S(1)} %convert_dynamic-update-slice_fusion), channel_id=1, replica_groups=mesh['vocab'=4,'dp'=2,'replica'=4] {'dp'}, use_global_device_ids=true, to_apply=%add | all-reduce | flops 16 | bytes 128
  43.1 0.1 fusion.5
  43.2 0.1 reshape.57
  43.3 0.0 copy-done
  43.3 4.6 %all_gather.7 = f32[16,1024]{1,0:T(8,128)S(1)} all-gather(f32[8,1024]{1,0:T(8,128)S(1)} %copy-done), channel_id=1, replica_groups=mesh['vocab'=4,'dp'=2,'replica'=4] {'dp'}, dimensions={0}, use_global_device_ids=true | all-gather | bytes 98304 | tf_op jit(solution)/shard_map/all_gather | solution.py:11
  47.9 0.0 collective-permute-done
  47.9 0.0 copy-done.1
  47.9 0.7 fusion
  48.6 0.1 add_power_fusion
  48.7 0.0 copy-start.2
  48.7 1.4 %fusion.7 = (f32[1024]{0:T(1024)}, bf16[256,1024]{1,0:T(8,128)(2,1)S(1)}) fusion(f32[16,1024]{1,0:T(8,128)S(1)} %broadcast_add_fusion, f32[16,1024]{1,0:T(8,128)S(1)} %get-tuple-element.22, f32[1024]{0:T(1024)S(1)} %copy-done.1, bf16[256,1024]{1,0:T(8,128)(2,1)S(1)} %collective-permute-done, bf16[256,1024]{1,0:T(8,128)(2,1)S(1)} %convolution_convert_fusion, ...), kind=kLoop, calls=%fused_computation.21 | loop fusion | flops 3668992 | bytes 1713152 | tf_op jit(solution)/shard_map/reduce_sum | solution.py:39
  50.1 4.9 %fusion.2 = f32[256,2048]{1,0:T(8,128)} fusion(bf16[2048,1024]{1,0:T(8,128)(2,1)} %param.6, bf16[256,1024]{1,0:T(8,128)(2,1)S(1)} %get-tuple-element.21), kind=kOutput, calls=%fused_computation.9 | convolution fusion | flops 1073741824 | bytes 6815744 | tf_op jit(solution)/shard_map/tv,kv->tk/dot_general | solution.py:41
  55.0 0.0 copy-done.2
  55.0 0.0 reduce-scatter.2.cloned.1.call-update
  55.0 4.5 %convolution_bitcast_fusion = f32[2048,1024]{0,1:T(8,128)} fusion(bf16[256,2048]{1,0:T(8,128)(2,1)S(1)} %bitcast.25, bf16[256,1024]{1,0:T(8,128)(2,1)S(1)} %get-tuple-element.21), kind=kOutput, calls=%fused_computation | convolution fusion | flops 1073741824 | bytes 9961472 | tf_op jit(solution)/shard_map/tk,tv->kv/dot_general | solution.py:43
  59.6 9.3 %copy.14 = f32[2048,1024]{1,0:T(8,128)} copy(f32[2048,1024]{0,1:T(8,128)} %convolution_bitcast_fusion) | data formatting | bytes 16777216
  68.9 0.6 constant_dynamic-slice_fusion
  69.5 48.0 %reduce-scatter.2.cloned.1.call-done = f32[16,2048]{1,0:T(8,128)} async-done(((f32[256,2048]{1,0:T(8,128)}), f32[16,2048]{1,0:T(8,128)}) %reduce-scatter.2.cloned.1.call-update) | async-done | bytes 131088 | tf_op jit(solution)/shard_map/reduce_scatter | solution.py:42
  (3 shorter events, 0.0 us)
Async XLA Ops:
  7.2 110.4 %reduce-scatter.2.cloned.1.call-start = ((), (), s32[]{:S(2)}) async-start(), calls=%async_computation.2 | async-start | bytes 2228224 | tf_op jit(solution)/shard_map/reduce_scatter | solution.py:42
  27.0 3.9 %copy-start.4 = (u32[32]{0:T(128)S(1)}, u32[32]{0:T(128)}, u32[]{:S(2)}) copy-start(u32[32]{0:T(128)} %constant.29) | copy-start | bytes 388
  27.0 5.1 %copy-start.3 = (s32[8]{0:T(128)S(1)}, s32[8]{0:T(128)}, u32[]{:S(2)}) copy-start(s32[8]{0:T(128)} %param.9) | copy-start | bytes 100
  27.0 16.3 %copy-start = (f32[8,1024]{1,0:T(8,128)S(1)}, f32[8,1024]{1,0:T(8,128)}, u32[]{:S(2)}) copy-start(f32[8,1024]{1,0:T(8,128)} %param.8) | copy-start | bytes 98308
  27.0 20.9 %copy-start.1 = (f32[1024]{0:T(1024)S(1)}, f32[1024]{0:T(1024)}, u32[]{:S(2)}) copy-start(f32[1024]{0:T(1024)} %param.7) | copy-start | bytes 12292
  30.5 17.4 %collective-permute-start = (bf16[256,1024]{1,0:T(8,128)(2,1)S(1)}, bf16[256,1024]{1,0:T(8,128)(2,1)S(1)}, u32[]{:S(2)}, u32[]{:S(2)}) collective-permute-start(bf16[256,1024]{1,0:T(8,128)(2,1)S(1)} %convolution_convert_fusion), channel_id=1, source_target_pairs={{0,4},{4,0},{1,5},{5,1},{2,6},{6,2},{3,7},{7,3},{8,12},{12,8},{9,1... | collective-permute-start | bytes 1572872 | tf_op jit(solution)/shard_map/ppermute | solution.py:19
  48.7 6.3 %copy-start.2 = (f32[1024]{0:T(1024)}, f32[1024]{0:T(1024)S(1)}, u32[]{:S(2)}) copy-start(f32[1024]{0:T(1024)S(1)} %broadcast_multiply_fusion) | copy-start | bytes 12292
Sparse Core Ops, SparseCore 0:
  55.2 62.3 reduce-scatter.1

commit v2 on v1

--- a/solution.py
+++ b/solution.py
@@ -1,6 +1,8 @@
 import jax
 import jax.numpy as jnp
 from jax import lax
+from jax.experimental import pallas as pl
+from jax.experimental.pallas import tpu as pltpu
 from jax.sharding import PartitionSpec as P
 
 
@@ -46,7 +48,250 @@
     return (pooled_own, term_mean, bias_grad, weight_grad, input_grad)
 
 
+NC = 4
+MESH = pl.DeviceIdType.MESH
+
+
+def head_kernel(
+    hidden, weight, bias, replen,
+    pooled_out, mean_out, biasg_out, cols_out, grad_out, inp_out,
+    wv, xall, rl, prt, rpt, factor, pool, grad, ipf, s1, r1, k2, s2, r2, k3, s3, r3,
+    w_sem, hs_send, hs_recv, fw_send, fw_recv, rl_send, rl_recv, pt_send, pt_recv,
+    c_send, c_recv, y_send, y_recv, z_send, z_recv,
+):
+    v, d, rz = lax.axis_index("vocab"), lax.axis_index("dp"), lax.axis_index("replica")
+    p = 1 - d
+    b, a = lax.rem(v, 2), v // 2
+    sib = {"vocab": v + 1 - 2 * b}
+    yp = {"vocab": lax.rem(v + 2, 4)}
+    dpp = {"dp": p}
+    half = hidden.shape[1] // 2
+    cw = half // NC
+    vw = wv.shape[1] // NC
+    rows = hidden.shape[0]
+    seqs = rl.shape[1]
+    slen = rows // seqs
+    hr = rows // 4
+
+    def remote(src, dst, ss, rs, dev):
+        return pltpu.make_async_remote_copy(
+            src_ref=src, dst_ref=dst, send_sem=ss, recv_sem=rs, device_id=dev, device_id_type=MESH
+        )
+
+    loads = []
+    for c in range(NC):
+        cp = pltpu.make_async_copy(
+            weight.at[:, pl.ds(c * vw, vw)], wv.at[:, pl.ds(c * vw, vw)], w_sem.at[c]
+        )
+        cp.start()
+        loads.append(cp)
+    barrier = pltpu.get_barrier_semaphore()
+    zps = [{"replica": lax.rem(rz + j, 4)} for j in (1, 2, 3)]
+    for dev in [sib, yp, dpp] + zps:
+        pl.semaphore_signal(barrier, inc=1, device_id=dev, device_id_type=MESH)
+    pl.semaphore_wait(barrier, 6)
+
+    pend = []
+    hcopies = []
+    for q in range(2):
+        rr = pl.ds(pl.multiple_of(b * (2 * hr) + q * hr, hr), hr)
+        cp = remote(
+            hidden.at[rr, pl.ds(pl.multiple_of(p * half, half), half)],
+            xall.at[d, rr], hs_send.at[q], hs_recv.at[q], dpp,
+        )
+        cp.start()
+        hcopies.append(cp)
+    rlc = remote(replen, rl.at[d], rl_send, rl_recv, dpp)
+    rlc.start()
+    pend += hcopies + [rlc]
+    rl[d] = replen[...]
+    xall[d] = hidden[:, pl.ds(pl.multiple_of(d * half, half), half)]
+
+    def parts(h, ph):
+        out = []
+        for c in range(NC):
+            if ph == 0:
+                loads[c].wait()
+            prt[h, c] = jnp.dot(
+                xall[h], wv[:, c * vw : (c + 1) * vw], preferred_element_type=jnp.float32
+            ).astype(jnp.bfloat16)
+            cp = remote(prt.at[h, c], rpt.at[h, c], pt_send.at[ph, c], pt_recv.at[ph, c], dpp)
+            cp.start()
+            out.append(cp)
+        return out
+
+    own_parts = parts(d, 0)
+    fws = []
+    for q in range(2):
+        hcopies[q].wait_recv()
+        rr = pl.ds(pl.multiple_of(b * (2 * hr) + q * hr, hr), hr)
+        cp = remote(xall.at[p, rr], xall.at[p, rr], fw_send.at[q], fw_recv.at[q], sib)
+        cp.start()
+        fws.append(cp)
+    for cp in fws:
+        cp.wait_recv()
+    other_parts = parts(p, 1)
+    pend += fws + own_parts + other_parts
+    rlc.wait_recv()
+
+    slot = lax.broadcasted_iota(jnp.int32, (seqs, slen, vw), 1).astype(jnp.float32)
+
+    def forward(h, c):
+        x = prt[h, c].astype(jnp.float32) + rpt[h, c].astype(jnp.float32)
+        x = x + bias[:, c * vw : (c + 1) * vw]
+        pos = jnp.maximum(x, 0.0)
+        act = jnp.log1p(pos).reshape(seqs, slen, vw)
+        lens = rl[h, :, wv.shape[1] :]
+        live = slot < lens[:, None, :]
+        act = jnp.where(live, act, 0.0)
+        sq = act * act
+        total = 1.0 + jnp.sum(sq * sq, axis=1)
+        root = jnp.sqrt(jnp.sqrt(total))
+        pool[h, c] = root - 1.0
+        inv = 1.0 / root
+        inv3 = inv * inv * inv
+        f = sq * act * inv3[:, None, :] / (1.0 + pos.reshape(seqs, slen, vw))
+        factor[h, c] = f.reshape(rows, vw)
+
+    for c in range(NC):
+        own_parts[c].wait_recv()
+        forward(p, c)
+    for c in range(NC):
+        other_parts[c].wait_recv()
+        forward(d, c)
+        cs = slice(c * vw, (c + 1) * vw)
+        mean = (
+            jnp.sum(pool[0, c], axis=0, keepdims=True) + jnp.sum(pool[1, c], axis=0, keepdims=True)
+        ) / (2 * seqs)
+        mean_out[:, cs] = mean
+        pooled_out[:, cs] = pool[d, c]
+        bsum = jnp.zeros((1, vw), jnp.float32)
+        for h in range(2):
+            gp = rl[h, :, cs] + mean
+            g = (factor[h, c].reshape(seqs, slen, vw) * gp[:, None, :]).reshape(rows, vw)
+            bsum = bsum + jnp.sum(g, axis=0, keepdims=True)
+            grad[h, :, cs] = g.astype(jnp.bfloat16)
+        biasg_out[:, cs] = bsum
+
+    vr = 2 * rows // 4
+    zr = vr // 4
+    cc, yy, zz = [], [], []
+    for c in range(NC):
+        res = lax.dot_general(
+            grad[...].reshape(2 * rows, NC * vw), wv[c * cw : (c + 1) * cw, :],
+            (((1,), (1,)), ((), ())), preferred_element_type=jnp.float32,
+        )
+        for u in range(4):
+            blk = res[u * vr : (u + 1) * vr]
+            ipf[c, u % 2, u // 2] = blk
+            s1[c, u % 2, u // 2] = blk.astype(jnp.bfloat16)
+        cp = remote(s1.at[c, 1 - b], r1.at[c], c_send.at[c], c_recv.at[c], sib)
+        cp.start()
+        cc.append(cp)
+    for c in range(NC):
+        cc[c].wait_recv()
+        s2[c] = (ipf[c, b, 1 - a] + r1[c, 1 - a].astype(jnp.float32)).astype(jnp.bfloat16)
+        cp = remote(s2.at[c], r2.at[c], y_send.at[c], y_recv.at[c], yp)
+        cp.start()
+        yy.append(cp)
+        k2[c] = ipf[c, b, a] + r1[c, a].astype(jnp.float32)
+    cols_out[...] = xall[...]
+    grad_out[...] = grad[...]
+    for c in range(NC):
+        yy[c].wait_recv()
+        tot = (k2[c] + r2[c].astype(jnp.float32)).reshape(4, zr, cw)
+        k3[c] = tot
+        s3[c] = tot.astype(jnp.bfloat16)
+        row = []
+        for j in (1, 2, 3):
+            to = lax.rem(rz + j, 4)
+            cp = remote(
+                s3.at[c, to], r3.at[c, j - 1], z_send.at[c, j - 1], z_recv.at[c, j - 1],
+                {"replica": to},
+            )
+            cp.start()
+            row.append(cp)
+        zz.append(row)
+    for c in range(NC):
+        tot = k3[c, rz]
+        for j in range(3):
+            zz[c][j].wait_recv()
+            tot = tot + r3[c, j].astype(jnp.float32)
+        inp_out[:, c * cw : (c + 1) * cw] = tot
+    for cp in pend + cc + yy + sum(zz, []):
+        cp.wait_send()
+
+
+def weight_kernel(cols, grad, out):
+    out[...] = lax.dot_general(
+        cols[...], grad[...], (((0,), (0,)), ((), ())), preferred_element_type=jnp.float32
+    )
+
+
+def fused(hidden, head_weight, head_bias, rep_cotangent, lengths):
+    rows, width = hidden.shape
+    half, vc = head_weight.shape
+    seqs = lengths.shape[0]
+    vw, cw = vc // NC, half // NC
+    vr = 2 * rows // 4
+    zr = vr // 4
+    bf, f32 = jnp.bfloat16, jnp.float32
+    wide = jnp.broadcast_to(lengths.astype(f32)[:, None], (seqs, vw))
+    replen = jnp.concatenate([rep_cotangent, wide], axis=1)
+    vm = pl.BlockSpec(memory_space=pltpu.VMEM)
+    dma = pltpu.SemaphoreType.DMA
+    sds = jax.ShapeDtypeStruct
+    pooled, mean, biasg, cols, grad, inp = pl.pallas_call(
+        head_kernel,
+        out_shape=(
+            sds((seqs, vc), f32), sds((1, vc), f32), sds((1, vc), f32),
+            sds((2, rows, half), bf), sds((2, rows, vc), bf), sds((zr, half), f32),
+        ),
+        in_specs=[vm, pl.BlockSpec(memory_space=pl.ANY), vm, vm],
+        out_specs=(vm,) * 6,
+        scratch_shapes=[
+            pltpu.VMEM((half, vc), bf),
+            pltpu.VMEM((2, rows, half), bf),
+            pltpu.VMEM((2, seqs, vc + vw), f32),
+            pltpu.VMEM((2, NC, rows, vw), bf),
+            pltpu.VMEM((2, NC, rows, vw), bf),
+            pltpu.VMEM((2, NC, rows, vw), f32),
+            pltpu.VMEM((2, NC, seqs, vw), f32),
+            pltpu.VMEM((2, rows, vc), bf),
+            pltpu.VMEM((NC, 2, 2, vr, cw), f32),
+            pltpu.VMEM((NC, 2, 2, vr, cw), bf),
+            pltpu.VMEM((NC, 2, vr, cw), bf),
+            pltpu.VMEM((NC, vr, cw), f32),
+            pltpu.VMEM((NC, vr, cw), bf),
+            pltpu.VMEM((NC, vr, cw), bf),
+            pltpu.VMEM((NC, 4, zr, cw), f32),
+            pltpu.VMEM((NC, 4, zr, cw), bf),
+            pltpu.VMEM((NC, 3, zr, cw), bf),
+            dma((NC,)), dma((2,)), dma((2,)), dma((2,)), dma((2,)), dma, dma,
+            dma((2, NC)), dma((2, NC)), dma((NC,)), dma((NC,)), dma((NC,)), dma((NC,)),
+            dma((NC, 3)), dma((NC, 3)),
+        ],
+        compiler_params=pltpu.CompilerParams(
+            collective_id=0, has_side_effects=True, vmem_limit_bytes=44 * 1024 * 1024
+        ),
+    )(hidden, head_weight, head_bias[None, :], replen)
+    kb = 256
+    weight_grad = pl.pallas_call(
+        weight_kernel,
+        grid=(half // kb,),
+        out_shape=sds((half, vc), f32),
+        in_specs=[
+            pl.BlockSpec((2 * rows, kb), lambda i: (0, i)),
+            pl.BlockSpec((2 * rows, vc), lambda i: (0, 0)),
+        ],
+        out_specs=pl.BlockSpec((kb, vc), lambda i: (i, 0)),
+        compiler_params=pltpu.CompilerParams(vmem_limit_bytes=24 * 1024 * 1024),
+    )(cols.reshape(2 * rows, half), grad.reshape(2 * rows, vc))
+    return (pooled, mean[0], biasg[0], weight_grad, inp)
+
+
 def solution(mesh):
+    small = mesh.shape["dp"] == 2 and mesh.shape["vocab"] == 4 and mesh.shape["replica"] == 4
     placed = (
         P("dp", None),
         P("dp", ("vocab", "replica")),
@@ -55,7 +300,7 @@
         P("dp"),
     )
     return jax.shard_map(
-        per_device,
+        fused if small else per_device,
         mesh=mesh,
         in_specs=placed,
         out_specs=(

time: 125 us -> 53.2 us (0.43)
  waiting for transfers between devices: 48 us -> 0 us
  Pallas kernels: 0 us -> 44.2 us
  blocking collectives: 33.1 us -> 0 us
  between operations: 14.8 us -> 0.65 us
  matrix products: 12.9 us -> 0 us
  local copies, waits for them, and re-layouts: 12.8 us -> 6.63 us
    reduce_scatter x1 -> x0, waiting for transfers between devices: 48 us -> none  [per_device(): lax.psum_scatter(input_part, ('vocab', 'replica'), scatter_dimension=0, t...]
    pallas_call x0 -> x2, Pallas kernels: none -> 44.2 us  [the longest x1 38.6 us: fused(): pl.pallas_call(head_kernel, out_shape=(sds((seqs, vc), f32), sds((1, vc),...]
    all_to_all x1 -> x0, blocking collectives: 17.6 us -> none  [per_device(): lax.all_to_all(hidden, 'dp', split_axis=1, concat_axis=0, tiled=True)]
    dot_general x3 -> x0, matrix products: 12.9 us -> none  [the longest x1 4.92 us: per_device(): jnp.einsum('tv,kv->tk', grad_round, head_weight, preferred_element_type=j...]
    unnamed x1 -> x0, blocking collectives: 10.9 us -> none
    unnamed x14 -> x10, local copies, waits for them, and re-layouts: 11.6 us -> 6.55 us
    all_gather x1 -> x0, blocking collectives: 4.58 us -> none  [per_device(): rep_all = lax.all_gather(rep_cotangent, 'dp', axis=0, tiled=True)]
    reduce_sum x2 -> x0, other arithmetic: 2.12 us -> none  [the longest x1 1.39 us: per_device(): bias_grad = jnp.sum(grad_logits, axis=0)]
  transfers between devices with their start and end apart: 2 -> 0, of which waited for: 1 -> 0; matrix products, arithmetic and copies ran while one was open for 12% -> 0% of each run, Pallas kernels for 0% -> 0%
where the time goes in v2:
time: 53.2 us; the launch traced here: 52.9 us
  Pallas kernels  44.2 us (83%)
  local copies, waits for them, and re-layouts  6.63 us (12%)
  other arithmetic  1.42 us (3%)
  between operations  0.65 us (1%)
    pallas_call x1, Pallas kernels, fused(): pl.pallas_call(head_kernel, out_shape=(sds((seqs, vc), f32), sds((1, vc),...  38.6 us
    unnamed x10, local copies, waits for them, and re-layouts  6.55 us
    pallas_call x1, Pallas kernels, fused(): pl.pallas_call(weight_kernel, grid=(half // kb,), out_shape=sds((half, vc...  5.64 us

profile of v2, /device:TPU:0, one launch (start us, length us, event | category | flops | bytes accessed | tf_op | source)
XLA Modules:
  0.0 52.9 jit_solution(14991023924424265589)
XLA Ops:
  0.6 0.7 %convert_element_type.3 = f32[8]{0:T(128)S(1)} convert(s32[8]{0:T(128)} %param.9) | non-fusion elementwise | flops 8 | bytes 64 | tf_op jit(solution)/shard_map/convert_element_type | solution.py:239
  1.3 0.1 broadcast_in_dim.10
  1.4 0.8 %pad_maximum_fusion.replen = f32[8,1280]{1,0:T(8,128)S(1)} fusion(f32[8,256]{1,0:T(8,128)S(1)} %broadcast_in_dim.10, f32[8,1024]{1,0:T(8,128)} %param.8), kind=kLoop, calls=%fused_computation | loop fusion | flops 10240 | bytes 81920 | tf_op jit(solution)/shard_map/concatenate | solution.py:240
  2.1 0.0 copy-start
  2.1 2.2 %copy-done = bf16[2048,1024]{1,0:T(8,128)(2,1)S(1)} copy-done((bf16[2048,1024]{1,0:T(8,128)(2,1)S(1)}, bf16[2048,1024]{1,0:T(8,128)(2,1)}, u32[]{:S(2)}) %copy-start) | copy-done | bytes 4194328
  4.3 0.0 copy-start.1
  4.3 1.2 %copy-done.1 = bf16[128,4096]{1,0:T(8,128)(2,1)S(1)} copy-done((bf16[128,4096]{1,0:T(8,128)(2,1)S(1)}, bf16[128,4096]{1,0:T(8,128)(2,1)}, u32[]{:S(2)}) %copy-start.1) | copy-done | bytes 1048600
  5.5 0.0 copy-start.2
  5.5 0.7 %copy-done.2 = f32[1024]{0:T(1024)S(1)} copy-done((f32[1024]{0:T(1024)S(1)}, f32[1024]{0:T(1024)}, u32[]{:S(2)}) %copy-start.2) | copy-done | bytes 4120
  6.2 38.6 %shard_map.92 = (f32[8,1024]{1,0:T(8,128)S(1)}, f32[1,1024]{1,0:T(1,128)S(1)}, f32[1,1024]{1,0:T(1,128)S(1)}, bf16[2,128,2048]{2,1,0:T(8,128)(2,1)S(1)}, bf16[2,...) custom-call(bf16[128,4096]{1,0:T(8,128)(2,1)S(1)} %copy-done.1, bf16[2048,1024]{1,0:T(8,128)(2,1)S(1)} %copy-done, ...), custom_call_target="tpu_custom_call" | custom-call | tf_op jit(solution)/shard_map/pallas_call | solution.py:244
  44.8 5.6 %shard_map.93 = f32[2048,1024]{1,0:T(8,128)} custom-call(bf16[256,2048]{1,0:T(8,128)(2,1)S(1)} %bitcast.5, bf16[256,1024]{1,0:T(8,128)(2,1)S(1)} %bitcast.6), custom_call_target="tpu_custom_call" | custom-call | tf_op jit(solution)/shard_map/pallas_call | solution.py:279
  50.5 0.6 %copy.14 = f32[8,1024]{1,0:T(8,128)} copy(f32[8,1024]{1,0:T(8,128)S(1)} %get-tuple-element.22) | data formatting | bytes 65536
  51.1 0.6 %copy.15 = f32[1024]{0:T(1024)} copy(f32[1024]{0:T(1024)S(1)} %bitcast.8) | data formatting | bytes 8192
  51.7 0.6 %copy.16 = f32[1024]{0:T(1024)} copy(f32[1024]{0:T(1024)S(1)} %bitcast.7) | data formatting | bytes 8192
  52.3 0.7 %copy.17 = f32[16,2048]{1,0:T(8,128)} copy(f32[16,2048]{1,0:T(8,128)S(1)} %get-tuple-element.26) | data formatting | bytes 262144
Async XLA Ops:
  2.1 2.2 %copy-start = (bf16[2048,1024]{1,0:T(8,128)(2,1)S(1)}, bf16[2048,1024]{1,0:T(8,128)(2,1)}, u32[]{:S(2)}) copy-start(bf16[2048,1024]{1,0:T(8,128)(2,1)} %weight.1) | copy-start | bytes 12582916
  4.3 1.2 %copy-start.1 = (bf16[128,4096]{1,0:T(8,128)(2,1)S(1)}, bf16[128,4096]{1,0:T(8,128)(2,1)}, u32[]{:S(2)}) copy-start(bf16[128,4096]{1,0:T(8,128)(2,1)} %hidden.1) | copy-start | bytes 3145732
  5.5 0.7 %copy-start.2 = (f32[1024]{0:T(1024)S(1)}, f32[1024]{0:T(1024)}, u32[]{:S(2)}) copy-start(f32[1024]{0:T(1024)} %param.7) | copy-start | bytes 12292

commit v3 on v2

--- a/solution.py
+++ b/solution.py
@@ -53,10 +53,10 @@
 
 
 def head_kernel(
-    hidden, weight, bias, replen,
+    hidden, weight, bias_in, replen, lengths,
     pooled_out, mean_out, biasg_out, cols_out, grad_out, inp_out,
-    wv, xall, rl, prt, rpt, factor, pool, grad, ipf, s1, r1, k2, s2, r2, k3, s3, r3,
-    w_sem, hs_send, hs_recv, fw_send, fw_recv, rl_send, rl_recv, pt_send, pt_recv,
+    wv, bias, xall, xt, rl, ln, prt, rpt, factor, pool, grad, ipf, s1, r1, k2, s2, r2, k3, s3, r3,
+    w_sem, l_sem, o_sem, hs_send, hs_recv, fw_send, fw_recv, fy_send, fy_recv, ys_send, ys_recv, ln_send, ln_recv, rl_send, rl_recv, pt_send, pt_recv,
     c_send, c_recv, y_send, y_recv, z_send, z_recv,
 ):
     v, d, rz = lax.axis_index("vocab"), lax.axis_index("dp"), lax.axis_index("replica")
@@ -71,13 +71,24 @@
     rows = hidden.shape[0]
     seqs = rl.shape[1]
     slen = rows // seqs
-    hr = rows // 4
+    hr = rows // 8
 
     def remote(src, dst, ss, rs, dev):
         return pltpu.make_async_remote_copy(
             src_ref=src, dst_ref=dst, send_sem=ss, recv_sem=rs, device_id=dev, device_id_type=MESH
         )
 
+    firsts = [
+        pltpu.make_async_copy(
+            hidden.at[:, pl.ds(pl.multiple_of(d * half, half), half)], xall.at[d], l_sem.at[0]
+        ),
+        pltpu.make_async_copy(replen, rl.at[d], l_sem.at[1]),
+        pltpu.make_async_copy(bias_in, bias, l_sem.at[2]),
+    ]
+    for cp in firsts:
+        cp.start()
+    for i in range(seqs):
+        ln[d, i : i + 1, :] = jnp.full((1, vw), lengths[i].astype(jnp.float32))
     loads = []
     for c in range(NC):
         cp = pltpu.make_async_copy(
@@ -93,19 +104,24 @@
 
     pend = []
     hcopies = []
+
+    def piece(who, q):
+        return pl.ds(pl.multiple_of(who * (2 * hr) + q * hr, hr), hr)
+
     for q in range(2):
-        rr = pl.ds(pl.multiple_of(b * (2 * hr) + q * hr, hr), hr)
         cp = remote(
-            hidden.at[rr, pl.ds(pl.multiple_of(p * half, half), half)],
-            xall.at[d, rr], hs_send.at[q], hs_recv.at[q], dpp,
+            hidden.at[piece(v, q), pl.ds(pl.multiple_of(p * half, half), half)],
+            xall.at[d, piece(v, q)], hs_send.at[q], hs_recv.at[q], dpp,
         )
         cp.start()
         hcopies.append(cp)
     rlc = remote(replen, rl.at[d], rl_send, rl_recv, dpp)
     rlc.start()
-    pend += hcopies + [rlc]
-    rl[d] = replen[...]
-    xall[d] = hidden[:, pl.ds(pl.multiple_of(d * half, half), half)]
+    lnc = remote(ln.at[d], ln.at[d], ln_send, ln_recv, dpp)
+    lnc.start()
+    pend += hcopies + [rlc, lnc]
+    for cp in firsts:
+        cp.wait()
 
     def parts(h, ph):
         out = []
@@ -121,18 +137,35 @@
         return out
 
     own_parts = parts(d, 0)
-    fws = []
+    fws, fys, fyy = [], [], []
+    yv = lax.rem(v + 2, 4)
     for q in range(2):
         hcopies[q].wait_recv()
-        rr = pl.ds(pl.multiple_of(b * (2 * hr) + q * hr, hr), hr)
-        cp = remote(xall.at[p, rr], xall.at[p, rr], fw_send.at[q], fw_recv.at[q], sib)
+        src = xall.at[p, piece(v, q)]
+        cp = remote(src, src, fy_send.at[q], fy_recv.at[q], yp)
+        cp.start()
+        fyy.append(cp)
+        cp = remote(src, src, fw_send.at[q], fw_recv.at[q], sib)
         cp.start()
         fws.append(cp)
-    for cp in fws:
+    for q in range(2):
+        fyy[q].wait_recv()
+        src = xall.at[p, piece(yv, q)]
+        cp = remote(src, src, ys_send.at[q], ys_recv.at[q], sib)
+        cp.start()
+        fys.append(cp)
+    for cp in fws + fys:
         cp.wait_recv()
     other_parts = parts(p, 1)
-    pend += fws + own_parts + other_parts
+    pend += fws + fys + fyy + own_parts + other_parts
     rlc.wait_recv()
+    lnc.wait_recv()
+    for h in range(2):
+        for k in range(NC):
+            ks = slice(k * cw, (k + 1) * cw)
+            xt[ks, h * rows : (h + 1) * rows] = xall[h, :, ks].T
+    cols_copy = pltpu.make_async_copy(xt, cols_out, o_sem.at[0])
+    cols_copy.start()
 
     slot = lax.broadcasted_iota(jnp.int32, (seqs, slen, vw), 1).astype(jnp.float32)
 
@@ -141,7 +174,7 @@
         x = x + bias[:, c * vw : (c + 1) * vw]
         pos = jnp.maximum(x, 0.0)
         act = jnp.log1p(pos).reshape(seqs, slen, vw)
-        lens = rl[h, :, wv.shape[1] :]
+        lens = ln[h]
         live = slot < lens[:, None, :]
         act = jnp.where(live, act, 0.0)
         sq = act * act
@@ -173,6 +206,8 @@
             grad[h, :, cs] = g.astype(jnp.bfloat16)
         biasg_out[:, cs] = bsum
 
+    grad_copy = pltpu.make_async_copy(grad, grad_out, o_sem.at[1])
+    grad_copy.start()
     vr = 2 * rows // 4
     zr = vr // 4
     cc, yy, zz = [], [], []
@@ -195,8 +230,6 @@
         cp.start()
         yy.append(cp)
         k2[c] = ipf[c, b, a] + r1[c, a].astype(jnp.float32)
-    cols_out[...] = xall[...]
-    grad_out[...] = grad[...]
     for c in range(NC):
         yy[c].wait_recv()
         tot = (k2[c] + r2[c].astype(jnp.float32)).reshape(4, zr, cw)
@@ -220,12 +253,19 @@
         inp_out[:, c * cw : (c + 1) * cw] = tot
     for cp in pend + cc + yy + sum(zz, []):
         cp.wait_send()
-
-
-def weight_kernel(cols, grad, out):
-    out[...] = lax.dot_general(
-        cols[...], grad[...], (((0,), (0,)), ((), ())), preferred_element_type=jnp.float32
-    )
+    cols_copy.wait()
+    grad_copy.wait()
+
+
+def weight_kernel(cols, grad, pooled, mean, biasg, inp, out, pooled_o, mean_o, biasg_o, inp_o):
+    out[...] = jnp.dot(cols[...], grad[...], preferred_element_type=jnp.float32)
+
+    @pl.when(pl.program_id(0) == 0)
+    def _():
+        pooled_o[...] = pooled[...]
+        mean_o[...] = mean[...]
+        biasg_o[...] = biasg[...]
+        inp_o[...] = inp[...]
 
 
 def fused(hidden, head_weight, head_bias, rep_cotangent, lengths):
@@ -236,23 +276,25 @@
     vr = 2 * rows // 4
     zr = vr // 4
     bf, f32 = jnp.bfloat16, jnp.float32
-    wide = jnp.broadcast_to(lengths.astype(f32)[:, None], (seqs, vw))
-    replen = jnp.concatenate([rep_cotangent, wide], axis=1)
     vm = pl.BlockSpec(memory_space=pltpu.VMEM)
+    hbm = pl.BlockSpec(memory_space=pl.ANY)
     dma = pltpu.SemaphoreType.DMA
     sds = jax.ShapeDtypeStruct
     pooled, mean, biasg, cols, grad, inp = pl.pallas_call(
         head_kernel,
         out_shape=(
             sds((seqs, vc), f32), sds((1, vc), f32), sds((1, vc), f32),
-            sds((2, rows, half), bf), sds((2, rows, vc), bf), sds((zr, half), f32),
+            sds((half, 2 * rows), bf), sds((2, rows, vc), bf), sds((zr, half), f32),
         ),
-        in_specs=[vm, pl.BlockSpec(memory_space=pl.ANY), vm, vm],
-        out_specs=(vm,) * 6,
+        in_specs=[hbm] * 4 + [pl.BlockSpec(memory_space=pltpu.SMEM)],
+        out_specs=(vm, vm, vm, hbm, hbm, vm),
         scratch_shapes=[
             pltpu.VMEM((half, vc), bf),
+            pltpu.VMEM((1, vc), f32),
             pltpu.VMEM((2, rows, half), bf),
-            pltpu.VMEM((2, seqs, vc + vw), f32),
+            pltpu.VMEM((half, 2 * rows), bf),
+            pltpu.VMEM((2, seqs, vc), f32),
+            pltpu.VMEM((2, seqs, vw), f32),
             pltpu.VMEM((2, NC, rows, vw), bf),
             pltpu.VMEM((2, NC, rows, vw), bf),
             pltpu.VMEM((2, NC, rows, vw), f32),
@@ -267,26 +309,30 @@
             pltpu.VMEM((NC, 4, zr, cw), f32),
             pltpu.VMEM((NC, 4, zr, cw), bf),
             pltpu.VMEM((NC, 3, zr, cw), bf),
-            dma((NC,)), dma((2,)), dma((2,)), dma((2,)), dma((2,)), dma, dma,
+            dma((NC,)), dma((3,)), dma((2,)), dma((2,)), dma((2,)), dma((2,)), dma((2,)),
+            dma((2,)), dma((2,)), dma((2,)), dma((2,)), dma, dma, dma, dma,
             dma((2, NC)), dma((2, NC)), dma((NC,)), dma((NC,)), dma((NC,)), dma((NC,)),
             dma((NC, 3)), dma((NC, 3)),
         ],
         compiler_params=pltpu.CompilerParams(
-            collective_id=0, has_side_effects=True, vmem_limit_bytes=44 * 1024 * 1024
+            collective_id=0, has_side_effects=True, vmem_limit_bytes=60 * 1024 * 1024
         ),
-    )(hidden, head_weight, head_bias[None, :], replen)
+    )(hidden, head_weight, head_bias[None, :], rep_cotangent, lengths)
     kb = 256
-    weight_grad = pl.pallas_call(
+    small = (pooled, mean, biasg, inp)
+    whole = [pl.BlockSpec(x.shape, lambda i: (0, 0)) for x in small]
+    weight_grad, pooled, mean, biasg, inp = pl.pallas_call(
         weight_kernel,
         grid=(half // kb,),
-        out_shape=sds((half, vc), f32),
+        out_shape=[sds((half, vc), f32)] + [sds(x.shape, f32) for x in small],
         in_specs=[
-            pl.BlockSpec((2 * rows, kb), lambda i: (0, i)),
+            pl.BlockSpec((kb, 2 * rows), lambda i: (i, 0)),
             pl.BlockSpec((2 * rows, vc), lambda i: (0, 0)),
-        ],
-        out_specs=pl.BlockSpec((kb, vc), lambda i: (i, 0)),
-        compiler_params=pltpu.CompilerParams(vmem_limit_bytes=24 * 1024 * 1024),
-    )(cols.reshape(2 * rows, half), grad.reshape(2 * rows, vc))
+        ]
+        + whole,
+        out_specs=[pl.BlockSpec((kb, vc), lambda i: (i, 0))] + whole,
+        compiler_params=pltpu.CompilerParams(vmem_limit_bytes=60 * 1024 * 1024),
+    )(cols, grad.reshape(2 * rows, vc), *small)
     return (pooled, mean[0], biasg[0], weight_grad, inp)
 
 

time: 53.2 us -> 45.9 us (0.86)
  local copies, waits for them, and re-layouts: 6.63 us -> 0 us
  other arithmetic: 1.42 us -> 0 us
  Pallas kernels: 44.2 us -> 44.9 us
    unnamed x10 -> x0, local copies, waits for them, and re-layouts: 6.55 us -> none
    pallas_call x1, Pallas kernels: 5.64 us -> 7.62 us  [fused(): pl.pallas_call(weight_kernel, grid=(half // kb,), out_shape=[sds((half, v...]
    pallas_call x1, Pallas kernels: 38.6 us -> 37.3 us  [fused(): pl.pallas_call(head_kernel, out_shape=(sds((seqs, vc), f32), sds((1, vc),...]
    concatenate x1 -> x0, other arithmetic: 0.76 us -> none  [fused(): replen = jnp.concatenate([rep_cotangent, wide], axis=1)]
    convert_element_type x1 -> x0, other arithmetic: 0.66 us -> none  [fused(): wide = jnp.broadcast_to(lengths.astype(f32)[:, None], (seqs, vw))]
where the time goes in v3:
time: 45.9 us; the launch traced here: 45.6 us
  Pallas kernels  44.9 us (98%)
  between operations  0.64 us (1%)
    pallas_call x1, Pallas kernels, fused(): pl.pallas_call(head_kernel, out_shape=(sds((seqs, vc), f32), sds((1, vc),...  37.3 us
    pallas_call x1, Pallas kernels, fused(): pl.pallas_call(weight_kernel, grid=(half // kb,), out_shape=[sds((half, v...  7.62 us

profile of v3, /device:TPU:0, one launch (start us, length us, event | category | flops | bytes accessed | tf_op | source)
XLA Modules:
  0.0 45.6 jit_solution(8077002259278463580)
XLA Ops:
  0.6 37.3 %shard_map.92 = (f32[8,1024]{1,0:T(8,128)}, f32[1,1024]{1,0:T(1,128)}, f32[1,1024]{1,0:T(1,128)}, bf16[2048,256]{1,0:T(8,128)(2,1)}, bf16[2,128,1024]{2,1,0:T(8,128)(2,1)}, /*index=5*/f32[16,2048]{1,0:T(8,128)}) custom-call(bf16[128,4096]{1,0:T(8,128)(2,1)} %hidden.1, bf16[2048,1024]{1,0:T(8,128)(2,1)} %weight.1, f32[1,1024]{1,0:T(1,128)} %bitcast.5, ...), custom_call_target="tpu_custom_call" | custom-call | tf_op jit(solution)/shard_map/pallas_call | solution.py:283
  38.0 7.6 %shard_map.93 = (f32[2048,1024]{1,0:T(8,128)}, f32[8,1024]{1,0:T(8,128)}, f32[1,1024]{1,0:T(1,128)}, f32[1,1024]{1,0:T(1,128)}, f32[16,2048]{1,0:T(8,128)}) custom-call(bf16[2048,256]{1,0:T(8,128)(2,1)} %get-tuple-element.16.cols, bf16[256,1024]{1,0:T(8,128)(2,1)} %bitcast.4, f32[8,1024]{1,0:T(8,128)} %get-tuple-element.18.pooled, ...), custom_call_target="tpu_custom_call" | custom-call | tf_op jit(solution)/shard_map/pallas_call | solution.py:324

commit v4 on v3

--- a/solution.py
+++ b/solution.py
@@ -258,7 +258,9 @@
 
 
 def weight_kernel(cols, grad, pooled, mean, biasg, inp, out, pooled_o, mean_o, biasg_o, inp_o):
-    out[...] = jnp.dot(cols[...], grad[...], preferred_element_type=jnp.float32)
+    kb = out.shape[0]
+    at = pl.ds(pl.multiple_of(pl.program_id(0) * kb, kb), kb)
+    out[...] = jnp.dot(cols[at, :], grad[...], preferred_element_type=jnp.float32)
 
     @pl.when(pl.program_id(0) == 0)
     def _():
@@ -277,7 +279,7 @@
     zr = vr // 4
     bf, f32 = jnp.bfloat16, jnp.float32
     vm = pl.BlockSpec(memory_space=pltpu.VMEM)
-    hbm = pl.BlockSpec(memory_space=pl.ANY)
+    hbm = pl.BlockSpec(memory_space=pltpu.HBM)
     dma = pltpu.SemaphoreType.DMA
     sds = jax.ShapeDtypeStruct
     pooled, mean, biasg, cols, grad, inp = pl.pallas_call(
@@ -287,7 +289,7 @@
             sds((half, 2 * rows), bf), sds((2, rows, vc), bf), sds((zr, half), f32),
         ),
         in_specs=[hbm] * 4 + [pl.BlockSpec(memory_space=pltpu.SMEM)],
-        out_specs=(vm, vm, vm, hbm, hbm, vm),
+        out_specs=(vm,) * 6,
         scratch_shapes=[
             pltpu.VMEM((half, vc), bf),
             pltpu.VMEM((1, vc), f32),
@@ -315,7 +317,7 @@
             dma((NC, 3)), dma((NC, 3)),
         ],
         compiler_params=pltpu.CompilerParams(
-            collective_id=0, has_side_effects=True, vmem_limit_bytes=60 * 1024 * 1024
+            collective_id=0, has_side_effects=True, vmem_limit_bytes=52 * 1024 * 1024
         ),
     )(hidden, head_weight, head_bias[None, :], rep_cotangent, lengths)
     kb = 256
@@ -325,13 +327,9 @@
         weight_kernel,
         grid=(half // kb,),
         out_shape=[sds((half, vc), f32)] + [sds(x.shape, f32) for x in small],
-        in_specs=[
-            pl.BlockSpec((kb, 2 * rows), lambda i: (i, 0)),
-            pl.BlockSpec((2 * rows, vc), lambda i: (0, 0)),
-        ]
-        + whole,
+        in_specs=[vm] * 6,
         out_specs=[pl.BlockSpec((kb, vc), lambda i: (i, 0))] + whole,
-        compiler_params=pltpu.CompilerParams(vmem_limit_bytes=60 * 1024 * 1024),
+        compiler_params=pltpu.CompilerParams(vmem_limit_bytes=40 * 1024 * 1024),
     )(cols, grad.reshape(2 * rows, vc), *small)
     return (pooled, mean[0], biasg[0], weight_grad, inp)
 

time: 45.9 us -> 45.2 us (0.985)
  Pallas kernels: 44.9 us -> 42.2 us
  local copies, waits for them, and re-layouts: 0 us -> 2.09 us
    pallas_call x1, Pallas kernels: 7.62 us -> 5.49 us  [fused(): pl.pallas_call(weight_kernel, grid=(half // kb,), out_shape=[sds((half, v...]
    unnamed x0 -> x6, local copies, waits for them, and re-layouts: none -> 2.09 us
    pallas_call x1, Pallas kernels: 37.3 us -> 36.7 us  [fused(): pl.pallas_call(head_kernel, out_shape=(sds((seqs, vc), f32), sds((1, vc),...]
where the time goes in v4:
time: 45.2 us; the launch traced here: 44.9 us
  Pallas kernels  42.2 us (93%)
  local copies, waits for them, and re-layouts  2.09 us (5%)
  between operations  0.65 us (1%)
    pallas_call x1, Pallas kernels, fused(): pl.pallas_call(head_kernel, out_shape=(sds((seqs, vc), f32), sds((1, vc),...  36.7 us
    pallas_call x1, Pallas kernels, fused(): pl.pallas_call(weight_kernel, grid=(half // kb,), out_shape=[sds((half, v...  5.49 us
    unnamed x6, local copies, waits for them, and re-layouts  2.09 us

profile of v4, /device:TPU:0, one launch (start us, length us, event | category | flops | bytes accessed | tf_op | source)
XLA Modules:
  0.0 44.9 jit_solution(10450780860254821942)
XLA Ops:
  0.6 0.0 copy-start
  0.6 0.7 %copy-done = f32[8,1024]{1,0:T(8,128)S(1)} copy-done((f32[8,1024]{1,0:T(8,128)S(1)}, f32[8,1024]{1,0:T(8,128)}, u32[]{:S(2)}) %copy-start) | copy-done | bytes 32792
  1.4 0.0 copy-start.1
  1.4 0.7 %copy-done.1 = f32[1024]{0:T(1024)S(1)} copy-done((f32[1024]{0:T(1024)S(1)}, f32[1024]{0:T(1024)}, u32[]{:S(2)}) %copy-start.1) | copy-done | bytes 4120
  2.1 0.0 copy-start.2
  2.1 0.7 %copy-done.2 = s32[8]{0:T(128)S(1)} copy-done((s32[8]{0:T(128)S(1)}, s32[8]{0:T(128)}, u32[]{:S(2)}) %copy-start.2) | copy-done | bytes 56
  2.7 36.7 %shard_map.92 = (f32[8,1024]{1,0:T(8,128)S(1)}, f32[1,1024]{1,0:T(1,128)S(1)}, f32[1,1024]{1,0:T(1,128)S(1)}, bf16[2048,256]{1,0:T(8,128)(2,1)S(1)}, bf16[2,128,...) custom-call(bf16[128,4096]{1,0:T(8,128)(2,1)} %hidden.1, bf16[2048,1024]{1,0:T(8,128)(2,1)} %weight.1, ...), custom_call_target="tpu_custom_call" | custom-call | tf_op jit(solution)/shard_map/pallas_call | solution.py:285
  39.5 5.5 %shard_map.93 = (f32[2048,1024]{1,0:T(8,128)}, f32[8,1024]{1,0:T(8,128)}, f32[1,1024]{1,0:T(1,128)}, f32[1,1024]{1,0:T(1,128)}, f32[16,2048]{1,0:T(8,128)}) custom-call(bf16[2048,256]{1,0:T(8,128)(2,1)S(1)} %get-tuple-element.16.cols, bf16[256,1024]{1,0:T(8,128)(2,1)S(1)} %bitcast.4, f32[8,1024]{1,0:T(8,128)S(1)} %get-tuple-element.18.pooled, ...), custom_call_target="tpu_custom_call" | custom-call | tf_op jit(solution)/shard_map/pallas_call | solution.py:326
Async XLA Ops:
  0.6 0.8 %copy-start = (f32[8,1024]{1,0:T(8,128)S(1)}, f32[8,1024]{1,0:T(8,128)}, u32[]{:S(2)}) copy-start(f32[8,1024]{1,0:T(8,128)} %replen.1) | copy-start | bytes 98308
  1.4 0.7 %copy-start.1 = (f32[1024]{0:T(1024)S(1)}, f32[1024]{0:T(1024)}, u32[]{:S(2)}) copy-start(f32[1024]{0:T(1024)} %param.7) | copy-start | bytes 12292
  2.1 0.7 %copy-start.2 = (s32[8]{0:T(128)S(1)}, s32[8]{0:T(128)}, u32[]{:S(2)}) copy-start(s32[8]{0:T(128)} %lengths.1) | copy-start | bytes 100

commit v5 on v4

--- a/solution.py
+++ b/solution.py
@@ -49,6 +49,7 @@
 
 
 NC = 4
+RC = 8
 MESH = pl.DeviceIdType.MESH
 
 
@@ -66,7 +67,7 @@
     yp = {"vocab": lax.rem(v + 2, 4)}
     dpp = {"dp": p}
     half = hidden.shape[1] // 2
-    cw = half // NC
+    cw = half // RC
     vw = wv.shape[1] // NC
     rows = hidden.shape[0]
     seqs = rl.shape[1]
@@ -161,7 +162,7 @@
     rlc.wait_recv()
     lnc.wait_recv()
     for h in range(2):
-        for k in range(NC):
+        for k in range(RC):
             ks = slice(k * cw, (k + 1) * cw)
             xt[ks, h * rows : (h + 1) * rows] = xall[h, :, ks].T
     cols_copy = pltpu.make_async_copy(xt, cols_out, o_sem.at[0])
@@ -211,7 +212,7 @@
     vr = 2 * rows // 4
     zr = vr // 4
     cc, yy, zz = [], [], []
-    for c in range(NC):
+    for c in range(RC):
         res = lax.dot_general(
             grad[...].reshape(2 * rows, NC * vw), wv[c * cw : (c + 1) * cw, :],
             (((1,), (1,)), ((), ())), preferred_element_type=jnp.float32,
@@ -223,14 +224,14 @@
         cp = remote(s1.at[c, 1 - b], r1.at[c], c_send.at[c], c_recv.at[c], sib)
         cp.start()
         cc.append(cp)
-    for c in range(NC):
+    for c in range(RC):
         cc[c].wait_recv()
         s2[c] = (ipf[c, b, 1 - a] + r1[c, 1 - a].astype(jnp.float32)).astype(jnp.bfloat16)
         cp = remote(s2.at[c], r2.at[c], y_send.at[c], y_recv.at[c], yp)
         cp.start()
         yy.append(cp)
         k2[c] = ipf[c, b, a] + r1[c, a].astype(jnp.float32)
-    for c in range(NC):
+    for c in range(RC):
         yy[c].wait_recv()
         tot = (k2[c] + r2[c].astype(jnp.float32)).reshape(4, zr, cw)
         k3[c] = tot
@@ -245,7 +246,7 @@
             cp.start()
             row.append(cp)
         zz.append(row)
-    for c in range(NC):
+    for c in range(RC):
         tot = k3[c, rz]
         for j in range(3):
             zz[c][j].wait_recv()
@@ -274,7 +275,7 @@
     rows, width = hidden.shape
     half, vc = head_weight.shape
     seqs = lengths.shape[0]
-    vw, cw = vc // NC, half // NC
+    vw, cw = vc // NC, half // RC
     vr = 2 * rows // 4
     zr = vr // 4
     bf, f32 = jnp.bfloat16, jnp.float32
@@ -302,19 +303,19 @@
             pltpu.VMEM((2, NC, rows, vw), f32),
             pltpu.VMEM((2, NC, seqs, vw), f32),
             pltpu.VMEM((2, rows, vc), bf),
-            pltpu.VMEM((NC, 2, 2, vr, cw), f32),
-            pltpu.VMEM((NC, 2, 2, vr, cw), bf),
-            pltpu.VMEM((NC, 2, vr, cw), bf),
-            pltpu.VMEM((NC, vr, cw), f32),
-            pltpu.VMEM((NC, vr, cw), bf),
-            pltpu.VMEM((NC, vr, cw), bf),
-            pltpu.VMEM((NC, 4, zr, cw), f32),
-            pltpu.VMEM((NC, 4, zr, cw), bf),
-            pltpu.VMEM((NC, 3, zr, cw), bf),
+            pltpu.VMEM((RC, 2, 2, vr, cw), f32),
+            pltpu.VMEM((RC, 2, 2, vr, cw), bf),
+            pltpu.VMEM((RC, 2, vr, cw), bf),
+            pltpu.VMEM((RC, vr, cw), f32),
+            pltpu.VMEM((RC, vr, cw), bf),
+            pltpu.VMEM((RC, vr, cw), bf),
+            pltpu.VMEM((RC, 4, zr, cw), f32),
+            pltpu.VMEM((RC, 4, zr, cw), bf),
+            pltpu.VMEM((RC, 3, zr, cw), bf),
             dma((NC,)), dma((3,)), dma((2,)), dma((2,)), dma((2,)), dma((2,)), dma((2,)),
             dma((2,)), dma((2,)), dma((2,)), dma((2,)), dma, dma, dma, dma,
-            dma((2, NC)), dma((2, NC)), dma((NC,)), dma((NC,)), dma((NC,)), dma((NC,)),
-            dma((NC, 3)), dma((NC, 3)),
+            dma((2, NC)), dma((2, NC)), dma((RC,)), dma((RC,)), dma((RC,)), dma((RC,)),
+            dma((RC, 3)), dma((RC, 3)),
         ],
         compiler_params=pltpu.CompilerParams(
             collective_id=0, has_side_effects=True, vmem_limit_bytes=52 * 1024 * 1024

time: 45.2 us -> 47.2 us (1.044)
  Pallas kernels: 42.2 us -> 44.2 us
    pallas_call x1, Pallas kernels: 36.7 us -> 38.7 us  [fused(): pl.pallas_call(head_kernel, out_shape=(sds((seqs, vc), f32), sds((1, vc),...]
where the time goes in v5:
time: 47.2 us; the launch traced here: 47 us
  Pallas kernels  44.2 us (94%)
  local copies, waits for them, and re-layouts  2.09 us (4%)
  between operations  0.65 us (1%)
    pallas_call x1, Pallas kernels, fused(): pl.pallas_call(head_kernel, out_shape=(sds((seqs, vc), f32), sds((1, vc),...  38.7 us
    pallas_call x1, Pallas kernels, fused(): pl.pallas_call(weight_kernel, grid=(half // kb,), out_shape=[sds((half, v...  5.49 us
    unnamed x6, local copies, waits for them, and re-layouts  2.09 us

profile of v5, /device:TPU:0, one launch (start us, length us, event | category | flops | bytes accessed | tf_op | source)
XLA Modules:
  0.0 47.0 jit_solution(8250522490322126458)
XLA Ops:
  0.6 0.0 copy-start
  0.6 0.7 %copy-done = f32[8,1024]{1,0:T(8,128)S(1)} copy-done((f32[8,1024]{1,0:T(8,128)S(1)}, f32[8,1024]{1,0:T(8,128)}, u32[]{:S(2)}) %copy-start) | copy-done | bytes 32792
  1.4 0.0 copy-start.1
  1.4 0.7 %copy-done.1 = f32[1024]{0:T(1024)S(1)} copy-done((f32[1024]{0:T(1024)S(1)}, f32[1024]{0:T(1024)}, u32[]{:S(2)}) %copy-start.1) | copy-done | bytes 4120
  2.1 0.0 copy-start.2
  2.1 0.7 %copy-done.2 = s32[8]{0:T(128)S(1)} copy-done((s32[8]{0:T(128)S(1)}, s32[8]{0:T(128)}, u32[]{:S(2)}) %copy-start.2) | copy-done | bytes 56
  2.7 38.7 %shard_map.92 = (f32[8,1024]{1,0:T(8,128)S(1)}, f32[1,1024]{1,0:T(1,128)S(1)}, f32[1,1024]{1,0:T(1,128)S(1)}, bf16[2048,256]{1,0:T(8,128)(2,1)S(1)}, bf16[2,128,...) custom-call(bf16[128,4096]{1,0:T(8,128)(2,1)} %hidden.1, bf16[2048,1024]{1,0:T(8,128)(2,1)} %weight.1, ...), custom_call_target="tpu_custom_call" | custom-call | tf_op jit(solution)/shard_map/pallas_call | solution.py:286
  41.5 5.5 %shard_map.93 = (f32[2048,1024]{1,0:T(8,128)}, f32[8,1024]{1,0:T(8,128)}, f32[1,1024]{1,0:T(1,128)}, f32[1,1024]{1,0:T(1,128)}, f32[16,2048]{1,0:T(8,128)}) custom-call(bf16[2048,256]{1,0:T(8,128)(2,1)S(1)} %get-tuple-element.16.cols, bf16[256,1024]{1,0:T(8,128)(2,1)S(1)} %bitcast.4, f32[8,1024]{1,0:T(8,128)S(1)} %get-tuple-element.18.pooled, ...), custom_call_target="tpu_custom_call" | custom-call | tf_op jit(solution)/shard_map/pallas_call | solution.py:327
Async XLA Ops:
  0.6 0.8 %copy-start = (f32[8,1024]{1,0:T(8,128)S(1)}, f32[8,1024]{1,0:T(8,128)}, u32[]{:S(2)}) copy-start(f32[8,1024]{1,0:T(8,128)} %replen.1) | copy-start | bytes 98308
  1.4 0.7 %copy-start.1 = (f32[1024]{0:T(1024)S(1)}, f32[1024]{0:T(1024)}, u32[]{:S(2)}) copy-start(f32[1024]{0:T(1024)} %param.7) | copy-start | bytes 12292
  2.1 0.7 %copy-start.2 = (s32[8]{0:T(128)S(1)}, s32[8]{0:T(128)}, u32[]{:S(2)}) copy-start(s32[8]{0:T(128)} %lengths.1) | copy-start | bytes 100
